TPU v7x, 32 devices: a whole 2x2x4 slice. The times are simulated.
32 devices in a mesh: blk: 8 (over y, x, core), exp: 4 (over z).
Axes of the slice: x: 2, y: 2, z: 4, core: 2. Of those that a mesh axis runs over, the one named last changes fastest.
Arguments:
- residual_deposit_sequence: bfloat16 [4, 1024, 1536], P('exp', 'blk'), may hold values from -60 to 60
- premix_rescaler: float32 [1536], replicated, may hold values from 0.25 to 1.75
- asking_projector: bfloat16 [1536, 1536], P(None, 'exp'), may hold values from -0.15625 to 0.15625
- lookup_projector: bfloat16 [1536, 512], P(None, 'exp'), may hold values from -0.15625 to 0.15625
- content_projector: bfloat16 [1536, 512], P(None, 'exp'), may hold values from -0.15625 to 0.15625
- final_projector: bfloat16 [1536, 1536], P('exp'), may hold values from -0.15625 to 0.15625
- logit_multipliers: float32 [12], replicated, may hold values from 1.5 to 6
- premixture_rescaler: float32 [1536], replicated, may hold values from 0.25 to 1.75
- specialist_switch_tensor: bfloat16 [8, 1536, 384], P('exp'), may hold values from -0.15625 to 0.15625
- specialist_widen_tensor: bfloat16 [8, 1536, 384], P('exp'), may hold values from -0.15625 to 0.15625
- specialist_shrink_tensor: bfloat16 [8, 384, 1536], P('exp'), may hold values from -0.3125 to 0.3125
- picked_specialist_labels: int32 [4, 1024, 2], P(None, 'blk'), may hold values from 0 to 7, all different within a row; in each aligned block of 128 rows (0 to 127, 128 to 255, ..., all dimensions but the last counted through in order) at most 64 rows name the same one
- specialist_shares: float32 [4, 1024, 2], P(None, 'blk'), may hold values from 0.1 to 1
Outputs:
- attention_update: bfloat16 [4, 1024, 1536], P('exp', 'blk')
- expert_update: bfloat16 [4, 1024, 1536], P('exp', 'blk')
Inputs may be any that keep to these rules, and one draw needn't show every extreme that they name: `picked_specialist_labels`: the 2 ids of a hit differ. Within each event's 128 hits on one index of blk (an aligned block of 128 rows) no expert is named by more than 64 hits, a bound that some block reaches.
All inputs are finite; a program needn't handle non-finite values.
Results may differ from a plain program's by a relative error of at most 0.019.
Values may be sent and summed in bfloat16 or wider, within the bound.
A program may use at most 192 MiB of HBM per device.

v0:
```python
import math
import jax
import jax.numpy as jnp
from jax import lax
from jax.sharding import PartitionSpec as P

D = 1536
PER_LANE_DIM = 128
TOP = 2
CAP = 64


def norm_rows(values, norm_gain):
    widened = values.astype(jnp.float32)
    return (
        widened * lax.rsqrt(jnp.mean(widened * widened, axis=-1, keepdims=True) + 1e-05) * norm_gain
    )


def head_norm(values):
    return values * lax.rsqrt(jnp.mean(values * values, axis=-1, keepdims=True) + 1e-06)


def attend_hits(
    rescaled_entries,
    asking_projector,
    lookup_projector,
    content_projector,
    final_projector,
    logit_multipliers,
):
    events, row_count, model_width = rescaled_entries.shape
    common_key_heads = lookup_projector.shape[1] // PER_LANE_DIM
    local_lane_count = asking_projector.shape[1] // PER_LANE_DIM
    askers_per_lookup = local_lane_count // common_key_heads
    query_heads = jnp.einsum(
        "std,de->ste", rescaled_entries, asking_projector, preferred_element_type=jnp.float32
    )
    query_heads = head_norm(
        query_heads.reshape(events, row_count, common_key_heads, askers_per_lookup, PER_LANE_DIM)
    ).astype(jnp.bfloat16)
    key_heads = jnp.einsum(
        "std,de->ste", rescaled_entries, lookup_projector, preferred_element_type=jnp.float32
    )
    key_heads = head_norm(
        key_heads.reshape(events, row_count, common_key_heads, PER_LANE_DIM)
    ).astype(jnp.bfloat16)
    value_heads = jnp.einsum(
        "std,de->ste", rescaled_entries, content_projector, preferred_element_type=jnp.float32
    )
    value_heads = value_heads.reshape(events, row_count, common_key_heads, PER_LANE_DIM).astype(
        jnp.bfloat16
    )
    inverse_root_dim = (logit_multipliers / math.sqrt(PER_LANE_DIM)).reshape(
        common_key_heads, askers_per_lookup
    )
    key_piece = lax.all_gather(key_heads, "blk", axis=1, tiled=True)
    value_piece = lax.all_gather(value_heads, "blk", axis=1, tiled=True)
    scores = jnp.einsum(
        "sikgd,sjkd->skgij", query_heads, key_piece, preferred_element_type=jnp.float32
    )
    expo = jnp.exp(scores * inverse_root_dim[None, :, :, None, None])
    totals = jnp.sum(expo, axis=-1)
    mixture = jnp.einsum(
        "skgij,sjkd->skgid",
        expo.astype(jnp.bfloat16),
        value_piece,
        preferred_element_type=jnp.float32,
    )
    totals, mixture = (totals, mixture)
    heads_out = head_norm(mixture / totals[..., None]).astype(jnp.bfloat16)
    out_blocks = final_projector.reshape(
        common_key_heads, askers_per_lookup, PER_LANE_DIM, model_width
    )
    return jnp.einsum("skgid,kgde->sie", heads_out, out_blocks, preferred_element_type=jnp.float32)


def slot_tables(chosen, expert_count):
    events, row_count, top_count = chosen.shape
    flat_ids = chosen.reshape(events, row_count * top_count)
    onehot = (
        flat_ids[:, :, None] == jnp.arange(expert_count, dtype=jnp.int32)[None, None, :]
    ).astype(jnp.int32)
    before = jnp.cumsum(onehot, axis=1) - onehot
    slot_of = jnp.sum(before * onehot, axis=2)
    source_rows = jnp.arange(row_count * top_count, dtype=jnp.int32)[None, :] // top_count
    event_index = jnp.arange(events, dtype=jnp.int32)[:, None]
    tables = (
        jnp.zeros((events, expert_count, CAP), jnp.int32)
        .at[event_index, flat_ids, slot_of]
        .set(source_rows)
    )
    return (slot_of, tables)


def run_experts(
    batched, specialist_switch_tensor, specialist_widen_tensor, specialist_shrink_tensor
):
    gate_act = jnp.einsum(
        "sjcd,jdf->sjcf", batched, specialist_switch_tensor, preferred_element_type=jnp.float32
    )
    up_act = jnp.einsum(
        "sjcd,jdf->sjcf", batched, specialist_widen_tensor, preferred_element_type=jnp.float32
    )
    hidden = (jax.nn.silu(gate_act) * up_act).astype(jnp.bfloat16)
    return jnp.einsum(
        "sjcf,jfd->sjcd", hidden, specialist_shrink_tensor, preferred_element_type=jnp.float32
    ).astype(jnp.bfloat16)


def body(
    residual_deposit_sequence,
    premix_rescaler,
    asking_projector,
    lookup_projector,
    content_projector,
    final_projector,
    logit_multipliers,
    premixture_rescaler,
    specialist_switch_tensor,
    specialist_widen_tensor,
    specialist_shrink_tensor,
    picked_specialist_labels,
    specialist_shares,
):
    specialist_slot = lax.axis_index("exp")
    exp_count = lax.axis_size("exp")
    rows_all = lax.all_gather(residual_deposit_sequence, "exp", axis=0, tiled=True)
    rescaled_entries = norm_rows(rows_all, premix_rescaler).astype(jnp.bfloat16)
    local_lane_count = asking_projector.shape[1] // PER_LANE_DIM
    device_scratch = lax.dynamic_slice_in_dim(
        logit_multipliers, specialist_slot * local_lane_count, local_lane_count
    )
    partial_out = attend_hits(
        rescaled_entries,
        asking_projector,
        lookup_projector,
        content_projector,
        final_projector,
        device_scratch,
    )
    attention_full = lax.psum_scatter(
        partial_out.astype(jnp.bfloat16), "exp", scatter_dimension=0, tiled=True
    ).astype(jnp.float32)
    attention_update = attention_full.astype(jnp.bfloat16)
    residual = residual_deposit_sequence.astype(jnp.float32) + attention_full
    expert_in = norm_rows(residual, premixture_rescaler).astype(jnp.bfloat16)
    row_count = expert_in.shape[1]
    local_experts = specialist_switch_tensor.shape[0]
    expert_count = local_experts * exp_count
    own_ids = lax.dynamic_slice_in_dim(picked_specialist_labels, specialist_slot, 1, 0)
    own_gates = lax.dynamic_slice_in_dim(specialist_shares, specialist_slot, 1, 0).reshape(
        row_count * TOP
    )
    slot_of, tables = slot_tables(own_ids, expert_count)
    outgoing = jnp.take(expert_in[0], tables[0].reshape(expert_count * CAP), axis=0)
    outgoing = outgoing.reshape(exp_count, local_experts, CAP, D)
    produced = run_experts(
        lax.all_to_all(outgoing, "exp", split_axis=0, concat_axis=0, tiled=True),
        specialist_switch_tensor,
        specialist_widen_tensor,
        specialist_shrink_tensor,
    )
    returned = lax.all_to_all(produced, "exp", split_axis=0, concat_axis=0, tiled=True)
    position = own_ids.reshape(row_count * TOP) * CAP + slot_of[0]
    values = jnp.take(returned.reshape(expert_count * CAP, D), position, axis=0).astype(jnp.float32)
    combined = jnp.sum((values * own_gates[:, None]).reshape(row_count, TOP, D), axis=1)
    expert_update = combined.astype(jnp.bfloat16)[None]
    return (attention_update, expert_update)


def solution(mesh):
    placed = (
        P("exp", "blk", None),
        P(),
        P(None, "exp"),
        P(None, "exp"),
        P(None, "exp"),
        P("exp", None),
        P(),
        P(),
        P("exp", None, None),
        P("exp", None, None),
        P("exp", None, None),
        P(None, "blk", None),
        P(None, "blk", None),
    )
    return jax.shard_map(
        body,
        mesh=mesh,
        in_specs=placed,
        out_specs=(P("exp", "blk", None), P("exp", "blk", None)),
        check_vma=False,
    )
```

profile of v0, /device:TPU:0, one launch (start us, length us, event | category | flops | bytes accessed | tf_op | source)
XLA Modules:
  0.0 258.9 jit_solution(3094345826512784104)
XLA Ops:
  8.0 41.4 %all-gather.6.cloned.1.call-done = bf16[4,128,1536]{2,1,0:T(8,128)(2,1)} async-done(((bf16[1,128,1536]{2,1,0:T(8,128)(2,1)}), bf16[4,128,1536]{2,1,0:T(8,128)(2,1)}) %all-gather.6.cloned.1.call-update) | async-done | bytes 1572880 | tf_op jit(solution)/shard_map/all_gather | solution.py:128
  49.4 1.9 fusion.1
  51.4 1.5 multiply_reduce_fusion.3
  52.9 0.7 multiply_convert_fusion.5
  53.7 2.7 %convolution_convert_fusion.1 = bf16[4,128,128]{2,1,0:T(8,128)(2,1)} fusion(bf16[4,128,1536]{2,1,0:T(8,128)(2,1)} %all-gather.6.cloned.1.call-done, f32[1536]{0:T(1024)S(1)} %copy-done.9, f32[4,128]{1,0:T(4,128)S(1)} %add_rsqrt_fusion.3, bf16[1536,128]{1,0:T(8,128)(2,1)S(1)} %copy-done.8), kind=kOutput, calls=%fused_computation.35 | convolution fusion | flops 204537856 | bytes 2105344 | tf_op jit(solution)/shard_map/std,de->ste/dot_general | solution.py:48
  56.6 3.7 %fusion.70 = (f32[4,128,384]{2,1,0:T(8,128)S(1)}, f32[4,128,384]{2,1,0:T(8,128)}) fusion(bf16[1536,384]{1,0:T(8,128)(2,1)} %param.15, bf16[4,128,1536]{2,1,0:T(8,128)(2,1)} %all-gather.6.cloned.1.call-done, f32[1536]{0:T(1024)S(1)} %copy-done.9, f32[4,128]{1,0:T(4,128)S(1)} %add_rsqrt_fusion.3), kind=kOutput, calls=%fused_computation.101 | convolution fusion | flops 607322112 | bytes 4333568 | tf_op jit(solution)/shard_map/std,de->ste/dot_general | solution.py:36
  60.2 1.1 copy.53
  61.4 1.4 copy.52
  62.8 1.2 reduce_sum.80
  64.0 12.2 %all-gather.8.cloned.1.call-done = bf16[4,1024,128]{1,2,0:T(8,128)(2,1)} async-done(((bf16[4,128,128]{1,2,0:T(8,128)(2,1)}), bf16[4,1024,128]{1,2,0:T(8,128)(2,1)}) %all-gather.8.cloned.1.call-update) | async-done | bytes 1048592 | tf_op jit(solution)/shard_map/all_gather | solution.py:57
  76.2 5.4 %bitcast_reduce_fusion = (f32[4,3,128]{2,1,0:T(4,128)S(1)}, f32[4,1024,128,3]{2,1,3,0:T(8,128)}) fusion(f32[3]{0:T(128)S(1)} %dynamic-slice_multiply_fusion, f32[4,128,3,128]{1,3,2,0:T(8,128)S(1)} %bitcast.150, f32[4,128,3]{1,2,0:T(4,128)S(1)} %add_rsqrt_fusion.1, bf16[4,1024,128]{1,2,0:T(8,128)(2,1)} %all-gather.8.cloned.1.call-done), kind=kOutput, calls=%fused_computation.3 | convolution fusion | flops 406190592 | bytes 8138764 | tf_op jit(solution)/shard_map/sikgd,sjkd->skgij/dot_general | solution.py:59
  81.6 20.6 %all-gather.10.cloned.1.call-done = bf16[4,1024,128]{2,1,0:T(8,128)(2,1)} async-done(((bf16[4,128,128]{2,1,0:T(8,128)(2,1)}), bf16[4,1024,128]{2,1,0:T(8,128)(2,1)}) %all-gather.10.cloned.1.call-update) | async-done | bytes 1048592 | tf_op jit(solution)/shard_map/all_gather | solution.py:58
  102.2 4.4 %multiply_reduce_fusion.2 = (f32[4,3,128]{2,1,0:T(4,128)S(1)}, f32[4,3,128,128]{2,3,1,0:T(8,128)S(1)}) fusion(f32[4,3,128]{2,1,0:T(4,128)S(1)} %get-tuple-element.8, bf16[4,1024,128]{2,1,0:T(8,128)(2,1)} %all-gather.10.cloned.1.call-done, f32[4,1024,128,3]{2,1,3,0:T(8,128)} %get-tuple-element.9, f32[3]{0:T(128)S(1)} %dynamic-slice_multiply_fusion), kind=kOutput, calls=%fused_computation.50 | convolution fusion | flops 406387200 | bytes 8138764 | tf_op jit(solution)/shard_map/skgij,sjkd->skgid/dot_general | solution.py:64
  106.7 2.2 fusion.8
  108.9 0.7 broadcast_multiply_fusion
  111.1 11.2 %scatter_fusion = s32[8,64]{1,0:T(8,128)S(1)} fusion(s32[8,64]{1,0:T(8,128)S(1)} %broadcast.318, s32[256]{0:T(256)S(1)} %bitcast.148, s32[256]{0:T(256)S(1)} %bitcast.159), kind=kCustom, calls=%fused_computation.2 | custom fusion | bytes 5120 | tf_op jit(solution)/shard_map/scatter | solution.py:91
  122.4 22.0 %reduce-scatter.2.cloned.1.call-done = bf16[1,128,1536]{2,1,0:T(8,128)(2,1)} async-done(((bf16[4,128,1536]{2,1,0:T(8,128)(2,1)}), bf16[1,128,1536]{2,1,0:T(8,128)(2,1)}) %reduce-scatter.2.cloned.1.call-update) | async-done | bytes 393232 | tf_op jit(solution)/shard_map/reduce_scatter | solution.py:142
  144.3 1.2 multiply_reduce_fusion.1
  145.6 1.2 fusion.60
  146.7 3.0 %gather_fusion = bf16[512,1536]{1,0:T(8,128)(2,1)} fusion(bf16[128,1536]{1,0:T(8,128)(2,1)S(1)} %fusion.60, s32[1024]{0:T(1024)S(1)} %pad_clamp_fusion.1), kind=kCustom, calls=%fused_computation | custom fusion | bytes 3147776 | tf_op jit(solution)/shard_map/jit(_take)/gather | solution.py:156
  149.7 1.6 broadcast_select_fusion
  151.3 39.7 %all_to_all.10 = bf16[4,2,64,1536]{3,2,1,0:T(8,128)(2,1)S(1)} all-to-all(bf16[4,2,64,1536]{3,2,1,0:T(8,128)(2,1)S(1)} %broadcast_select_fusion), channel_id=1, replica_groups=mesh['blk'=8,'exp'=4] {'exp'}, dimensions={0} | all-to-all | bytes 3145728 | tf_op jit(solution)/shard_map/all_to_all | solution.py:159
  191.0 1.1 copy-done.3
  192.1 1.0 fusion.17
  193.2 5.1 %fusion.9 = bf16[4,2,64,1536]{3,2,0,1:T(8,128)(2,1)} fusion(bf16[2,384,1536]{2,1,0:T(8,128)(2,1)S(1)} %copy-done, bf16[2,1536,384]{2,1,0:T(8,128)(2,1)} %param.22, bf16[4,2,64,1536]{3,2,1,0:T(8,128)(2,1)} %copy-done.3, f32[4,2,64,384]{3,2,0,1:T(8,128)S(1)} %fusion.17), kind=kOutput, calls=%fused_computation.18 | convolution fusion | flops 1209925632 | bytes 8650752 | tf_op jit(solution)/shard_map/sjcf,jfd->sjcd/dot_general | solution.py:106
  198.3 2.7 %copy.65 = bf16[4,2,64,1536]{3,2,1,0:T(8,128)(2,1)} copy(bf16[4,2,64,1536]{3,2,0,1:T(8,128)(2,1)} %fusion.9) | data formatting | bytes 3145728 | tf_op jit(solution)/shard_map/convert_element_type | solution.py:108
  200.9 4.3 %all-to-all-start.1 = ((bf16[4,2,64,1536]{3,2,1,0:T(8,128)(2,1)}), bf16[4,2,64,1536]{3,2,1,0:T(8,128)(2,1)}, u32[]{:S(2)}, u32[]{:S(2)}) async-start(bf16[4,2,64,1536]{3,2,1,0:T(8,128)(2,1)} %copy.65), calls=%async_computation.2 | async-start | bytes 3145728 | tf_op jit(solution)/shard_map/all_to_all | solution.py:164
  205.7 0.7 dynamic-slice_bitcast_fusion
  206.7 35.1 %all-to-all-done.1 = bf16[4,2,64,1536]{3,2,1,0:T(8,128)(2,1)} async-done(((bf16[4,2,64,1536]{3,2,1,0:T(8,128)(2,1)}), bf16[4,2,64,1536]{3,2,1,0:T(8,128)(2,1)}, u32[]{:S(2)}, u32[]{:S(2)}) %all-to-all-start.1) | async-done | bytes 1572896 | tf_op jit(solution)/shard_map/all_to_all | solution.py:164
  241.8 4.5 %gather_fusion.1 = bf16[256,1536]{1,0:T(8,128)(2,1)} fusion(bf16[512,1536]{1,0:T(8,128)(2,1)} %bitcast.38, s32[1024]{0:T(1024)S(1)} %pad_clamp_fusion), kind=kCustom, calls=%fused_computation.1 | custom fusion | bytes 1573888 | tf_op jit(solution)/shard_map/jit(_take)/gather | solution.py:166
  246.3 2.2 gather.15
  248.4 3.9 %multiply_reduce_fusion = bf16[128,1536]{1,0:T(8,128)(2,1)} fusion(bf16[128,2,1536]{2,1,0:T(2,128)(2,1)S(1)} %gather.15, pred[128,2]{1,0:T(8,128)(4,1)S(1)} %copy.61, f32[128,2]{1,0:T(8,128)S(1)} %copy.67), kind=kLoop, calls=%fused_computation.24 | loop fusion | flops 1376256 | bytes 1180928 | tf_op jit(solution)/shard_map/reduce_sum | solution.py:167
  (63 shorter events, 3.3 us)
Async XLA Ops:
  7.2 186.0 %copy-start = (bf16[2,384,1536]{2,1,0:T(8,128)(2,1)S(1)}, bf16[2,384,1536]{2,1,0:T(8,128)(2,1)}, u32[]{:S(2)}) copy-start(bf16[2,384,1536]{2,1,0:T(8,128)(2,1)} %param.23) | copy-start | bytes 7077892
  7.2 44.2 %copy-start.7 = (bf16[1536,128]{1,0:T(8,128)(2,1)S(1)}, bf16[1536,128]{1,0:T(8,128)(2,1)}, u32[]{:S(2)}) copy-start(bf16[1536,128]{1,0:T(8,128)(2,1)} %param.16) | copy-start | bytes 1179652
  7.2 42.2 %all-gather.6.cloned.1.call-start = ((), (), s32[]{:S(2)}) async-start(), calls=%async_computation.3 | async-start | bytes 1966080 | tf_op jit(solution)/shard_map/all_gather | solution.py:128
  7.9 68.3 %all-gather.8.cloned.1.call-start = ((), (), s32[]{:S(2)}) async-start(), calls=%async_computation.5 | async-start | bytes 1179648 | tf_op jit(solution)/shard_map/all_gather | solution.py:57
  49.4 1.9 copy-start.2
  51.4 2.3 copy-start.8
  51.4 2.3 copy-start.9
  53.6 2.9 %copy-start.10 = (f32[12]{0:T(128)S(1)}, f32[12]{0:T(128)}, u32[]{:S(2)}) copy-start(f32[12]{0:T(128)} %param.19) | copy-start | bytes 148
  53.6 48.6 %all-gather.10.cloned.1.call-start = ((), (), s32[]{:S(2)}) async-start(), calls=%async_computation.6 | async-start | bytes 1179648 | tf_op jit(solution)/shard_map/all_gather | solution.py:58
  56.4 87.9 %reduce-scatter.2.cloned.1.call-start = ((), (), s32[]{:S(2)}) async-start(), calls=%async_computation.4 | async-start | bytes 1966080 | tf_op jit(solution)/shard_map/reduce_scatter | solution.py:142
  102.2 4.5 %copy-start.4 = (bf16[384,1536]{1,0:T(8,128)(2,1)S(1)}, bf16[384,1536]{1,0:T(8,128)(2,1)}, u32[]{:S(2)}) copy-start(bf16[384,1536]{1,0:T(8,128)(2,1)} %param.18) | copy-start | bytes 3538948
  108.9 35.4 %copy-start.1 = (bf16[1,128,1536]{2,1,0:T(8,128)(2,1)S(1)}, bf16[1,128,1536]{2,1,0:T(8,128)(2,1)}, u32[]{:S(2)}) copy-start(bf16[1,128,1536]{2,1,0:T(8,128)(2,1)} %param.13) | copy-start | bytes 1179652
  110.0 35.5 %copy-start.5 = (f32[1536]{0:T(1024)S(1)}, f32[1536]{0:T(1024)}, u32[]{:S(2)}) copy-start(f32[1536]{0:T(1024)} %param.20) | copy-start | bytes 18436
  151.3 40.8 %copy-start.6 = (bf16[2,1536,384]{2,1,0:T(8,128)(2,1)S(1)}, bf16[2,1536,384]{2,1,0:T(8,128)(2,1)}, u32[]{:S(2)}) copy-start(bf16[2,1536,384]{2,1,0:T(8,128)(2,1)} %param.21) | copy-start | bytes 7077892
  191.0 1.1 copy-start.3
  200.9 40.9 %all-to-all-start.1 = ((bf16[4,2,64,1536]{3,2,1,0:T(8,128)(2,1)}), bf16[4,2,64,1536]{3,2,1,0:T(8,128)(2,1)}, u32[]{:S(2)}, u32[]{:S(2)}) async-start(bf16[4,2,64,1536]{3,2,1,0:T(8,128)(2,1)} %copy.65), calls=%async_computation.2 | async-start | bytes 3145728 | tf_op jit(solution)/shard_map/all_to_all | solution.py:164
Sparse Core Ops, SparseCore 0:
  9.6 39.7 all-gather.5
  53.8 22.4 all-gather.7
  78.7 23.4 all-gather.9
  109.0 35.2 reduce-scatter.1
where the time goes:
time: 260 us; the launch traced here: 259 us
  waiting for transfers between devices  132 us (51%)
  blocking collectives  39.7 us (15%)
  local copies, waits for them, and re-layouts  29.3 us (11%)
  matrix products  26 us (10%)
  between operations  14.1 us (5%)
  other arithmetic  13.3 us (5%)
  starting transfers between devices  4.49 us (2%)
    all_gather x1, waiting for transfers between devices, body(): lax.all_gather(residual_deposit_sequence, 'exp', axis=0, tiled=True)  41.4 us
    all_to_all x1, blocking collectives, body(): lax.all_to_all(outgoing, 'exp', split_axis=0, concat_axis=0, tiled=True)  39.7 us
    all_to_all x1, waiting for transfers between devices, body(): lax.all_to_all(produced, 'exp', split_axis=0, concat_axis=0, tiled=True)  35.1 us
    reduce_scatter x1, waiting for transfers between devices, body(): lax.psum_scatter(partial_out.astype(jnp.bfloat16), 'exp', scatter_dimensi...  22 us
    all_gather x1, waiting for transfers between devices, attend_hits(): value_piece = lax.all_gather(value_heads, 'blk', axis=1, tiled=True)  20.6 us
    all_gather x1, waiting for transfers between devices, attend_hits(): key_piece = lax.all_gather(key_heads, 'blk', axis=1, tiled=True)  12.2 us
    scatter x1, local copies, waits for them, and re-layouts, slot_tables(): tables = jnp.zeros((events, expert_count, CAP), jnp.int32).at[event_index...  11.2 us
    gather x2, local copies, waits for them, and re-layouts, body(): jnp.take(returned.reshape(expert_count * CAP, D), position, axis=0)  6.65 us
  transfers between devices with their start and end apart: 5, of which 5 were waited for; matrix products, arithmetic and copies ran while one was open for 12% of the time, Pallas kernels for 0%

commit v1 on v0

--- a/solution.py
+++ b/solution.py
@@ -55,7 +55,21 @@
         common_key_heads, askers_per_lookup
     )
     key_piece = lax.all_gather(key_heads, "blk", axis=1, tiled=True)
-    value_piece = lax.all_gather(value_heads, "blk", axis=1, tiled=True)
+    ways, here, turn = (lax.axis_size("blk"), lax.axis_index("blk"), value_heads.shape[1])
+    lengths = [n * ways if d == 1 else n for d, n in enumerate(value_heads.shape)]
+    full = lax.dynamic_update_slice_in_dim(
+        jnp.zeros(lengths, value_heads.dtype), value_heads, here * turn, axis=1
+    )
+    going_up = going_down = value_heads
+    for far in range(1, ways // 2 + 1):
+        going_up = lax.ppermute(going_up, "blk", [(d, (d + 1) % ways) for d in range(ways)])
+        full = lax.dynamic_update_slice_in_dim(full, going_up, (here - far) % ways * turn, axis=1)
+        if 2 * far < ways:
+            going_down = lax.ppermute(going_down, "blk", [(d, (d - 1) % ways) for d in range(ways)])
+            full = lax.dynamic_update_slice_in_dim(
+                full, going_down, (here + far) % ways * turn, axis=1
+            )
+    value_piece = full
     scores = jnp.einsum(
         "sikgd,sjkd->skgij", query_heads, key_piece, preferred_element_type=jnp.float32
     )

time: 260 us -> 242 us (0.931)
  waiting for transfers between devices: 132 us -> 104 us
  local copies, waits for them, and re-layouts: 29.3 us -> 40.2 us
  starting transfers between devices: 4.49 us -> 12.8 us
  matrix products: 26 us -> 18.4 us
    all_gather x1 -> x0, waiting for transfers between devices: 20.6 us -> none  [attend_hits(): value_piece = lax.all_gather(value_heads, 'blk', axis=1, tiled=True)]
    all_gather x1, waiting for transfers between devices: 12.2 us -> 0.01 us  [attend_hits(): key_piece = lax.all_gather(key_heads, 'blk', axis=1, tiled=True)]
    ppermute x0 -> x7, starting transfers between devices: none -> 8.37 us  [the longest x3 8.19 us: attend_hits(): lax.ppermute(going_down, 'blk', [(d, (d - 1) % ways) for d in range(ways)])]
    ppermute x0 -> x7, waiting for transfers between devices: none -> 5.29 us  [the longest x4 4.05 us: attend_hits(): lax.ppermute(going_up, 'blk', [(d, (d + 1) % ways) for d in range(ways)])]
    dynamic_update_slice x0 -> x8, local copies, waits for them, and re-layouts: none -> 4.87 us  [the longest x4 2.75 us: attend_hits(): lax.dynamic_update_slice_in_dim(full, going_up, (here - far) % ways * tur...]
    another operation x1 -> x9, local copies, waits for them, and re-layouts: 0.01 us -> 3.73 us
    dot_general x1, matrix products: 4.44 us -> 1.43 us  [attend_hits(): jnp.einsum('skgij,sjkd->skgid', expo.astype(jnp.bfloat16), value_piece, p...]
  transfers between devices with their start and end apart: 5 -> 11, of which waited for: 5 -> 7; matrix products, arithmetic and copies ran while one was open for 12% -> 13% of each run, Pallas kernels for 0% -> 0%
where the time goes in v1:
time: 242 us
  waiting for transfers between devices  104 us (43%)
  local copies, waits for them, and re-layouts  40.2 us (17%)
  blocking collectives  39.7 us (16%)
  matrix products  18.4 us (8%)
  between operations  14.3 us (6%)
  starting transfers between devices  12.8 us (5%)
  other arithmetic  12.2 us (5%)
    all_gather x1, waiting for transfers between devices, body(): lax.all_gather(residual_deposit_sequence, 'exp', axis=0, tiled=True)  41.3 us
    all_to_all x1, blocking collectives, body(): lax.all_to_all(outgoing, 'exp', split_axis=0, concat_axis=0, tiled=True)  39.7 us
    all_to_all x1, waiting for transfers between devices, body(): lax.all_to_all(produced, 'exp', split_axis=0, concat_axis=0, tiled=True)  35.4 us
    reduce_scatter x1, waiting for transfers between devices, body(): lax.psum_scatter(partial_out.astype(jnp.bfloat16), 'exp', scatter_dimensi...  21.4 us
    scatter x1, local copies, waits for them, and re-layouts, slot_tables(): tables = jnp.zeros((events, expert_count, CAP), jnp.int32).at[event_index...  11.2 us
    ppermute x3, starting transfers between devices, attend_hits(): lax.ppermute(going_down, 'blk', [(d, (d - 1) % ways) for d in range(ways)])  8.19 us
    gather x2, local copies, waits for them, and re-layouts, body(): jnp.take(returned.reshape(expert_count * CAP, D), position, axis=0)  6.66 us
    dot_general x1, matrix products, run_experts(): jnp.einsum('sjcf,jfd->sjcd', hidden, specialist_shrink_tensor, preferred_...  5.11 us
  transfers between devices with their start and end apart: 11, of which 7 were waited for; matrix products, arithmetic and copies ran while one was open for 13% of the time, Pallas kernels for 0%

profile of v1, /device:TPU:0, one launch (start us, length us, event | category | flops | bytes accessed | tf_op | source)
XLA Modules:
  0.0 241.7 jit_solution(1904841760679170357)
XLA Ops:
  8.1 41.3 %all-gather.4.cloned.1.call-done = bf16[4,128,1536]{2,1,0:T(8,128)(2,1)} async-done(((bf16[1,128,1536]{2,1,0:T(8,128)(2,1)}), bf16[4,128,1536]{2,1,0:T(8,128)(2,1)}) %all-gather.4.cloned.1.call-update) | async-done | bytes 1572880 | tf_op jit(solution)/shard_map/all_gather | solution.py:142
  49.4 1.9 fusion.1
  53.1 2.8 %convolution_convert_fusion.1 = bf16[4,128,128]{2,1,0:T(8,128)(2,1)} fusion(bf16[4,128,1536]{2,1,0:T(8,128)(2,1)} %all-gather.4.cloned.1.call-done, f32[1536]{0:T(1024)S(1)} %copy-done.13, f32[4,128]{1,0:T(4,128)S(1)} %add_rsqrt_fusion.3, bf16[1536,128]{1,0:T(8,128)(2,1)S(1)} %copy-done.12), kind=kOutput, calls=%fused_computation.35 | convolution fusion | flops 204537856 | bytes 2105344 | tf_op jit(solution)/shard_map/std,de->ste/dot_general | solution.py:48
  55.9 2.6 %collective-permute-start.1 = (bf16[4,128,1,128]{3,1,0,2:T(8,128)(2,1)}, bf16[4,128,1,128]{3,1,0,2:T(8,128)(2,1)S(1)}, u32[]{:S(2)}, u32[]{:S(2)}) collective-permute-start(bf16[4,128,1,128]{3,1,0,2:T(8,128)(2,1)} %bitcast.9), channel_id=1, source_target_pairs={{0,28},{4,0},{8,4},{12,8},{16,12},{20,16},{24,20},{28,24},{1,29},{... | collective-permute-start | bytes 393224 | tf_op jit(solution)/shard_map/ppermute | solution.py:68
  58.5 2.2 fusion.71
  60.7 1.4 copy.76
  62.2 1.0 copy.79
  64.5 1.4 copy.75
  66.9 2.7 %collective-permute-start.3 = (bf16[4,128,1,128]{3,1,0,2:T(8,128)(2,1)S(1)}, bf16[4,128,1,128]{3,1,0,2:T(8,128)(2,1)}, u32[]{:S(2)}, u32[]{:S(2)}) collective-permute-start(bf16[4,128,1,128]{3,1,0,2:T(8,128)(2,1)S(1)} %collective-permute-done.1), channel_id=1, source_target_pairs={{0,28},{4,0},{8,4},{12,8},{16,12},{20,16},{24,20},{28,24},{1,29},{... | collective-permute-start | bytes 393224 | tf_op jit(solution)/shard_map/ppermute | solution.py:68
  70.3 1.2 collective-permute-done.2
  73.3 1.0 copy.83
  74.3 2.9 %collective-permute-start.5 = (bf16[4,128,1,128]{3,1,0,2:T(8,128)(2,1)}, bf16[4,128,1,128]{3,1,0,2:T(8,128)(2,1)S(1)}, u32[]{:S(2)}, u32[]{:S(2)}) collective-permute-start(bf16[4,128,1,128]{3,1,0,2:T(8,128)(2,1)} %collective-permute-done.3), channel_id=1, source_target_pairs={{0,28},{4,0},{8,4},{12,8},{16,12},{20,16},{24,20},{28,24},{1,29},{... | collective-permute-start | bytes 393224 | tf_op jit(solution)/shard_map/ppermute | solution.py:68
  79.0 1.2 collective-permute-done.5
  81.0 2.6 %collective-permute-done.6 = bf16[4,128,1,128]{3,1,0,2:T(8,128)(2,1)} collective-permute-done((bf16[4,128,1,128]{3,1,0,2:T(8,128)(2,1)S(1)}, bf16[4,128,1,128]{3,1,0,2:T(8,128)(2,1)}, u32[]{:S(2)}, u32[]{:S(2)}) %collective-permute-start.6) | collective-permute-done | bytes 131104 | tf_op jit(solution)/shard_map/ppermute | solution.py:65
  85.4 2.9 %bitcast_reduce_fusion = (f32[4,3,128]{2,1,0:T(4,128)S(1)}, f32[4,1024,128,3]{2,1,3,0:T(8,128)S(1)}) fusion(f32[3]{0:T(128)S(1)} %dynamic-slice_multiply_fusion, f32[4,128,3,128]{1,3,2,0:T(8,128)S(1)} %bitcast.157, f32[4,128,3]{1,2,0:T(4,128)S(1)} %add_rsqrt_fusion.1, bf16[4,1024,128]{1,2,0:T(8,128)(2,1)} %all-gather.6.cloned.1.call-done), kind=kOutput, calls=%fused_computation.3 | convolution fusion | flops 406190592 | bytes 8138764 | tf_op jit(solution)/shard_map/sikgd,sjkd->skgij/dot_general | solution.py:73
  88.3 1.4 multiply_reduce_fusion.2
  89.8 2.2 fusion.8
  94.4 11.2 %scatter_fusion = s32[8,64]{1,0:T(8,128)S(1)} fusion(s32[8,64]{1,0:T(8,128)S(1)} %broadcast.333, s32[256]{0:T(256)S(1)} %bitcast.155, s32[256]{0:T(256)S(1)} %bitcast.170), kind=kCustom, calls=%fused_computation.2 | custom fusion | bytes 5120 | tf_op jit(solution)/shard_map/scatter | solution.py:105
  105.7 21.4 %reduce-scatter.2.cloned.1.call-done = bf16[1,128,1536]{2,1,0:T(8,128)(2,1)} async-done(((bf16[4,128,1536]{2,1,0:T(8,128)(2,1)}), bf16[1,128,1536]{2,1,0:T(8,128)(2,1)}) %reduce-scatter.2.cloned.1.call-update) | async-done | bytes 393232 | tf_op jit(solution)/shard_map/reduce_scatter | solution.py:156
  127.2 1.2 multiply_reduce_fusion.1
  128.4 1.2 fusion.60
  129.5 2.9 %gather_fusion = bf16[512,1536]{1,0:T(8,128)(2,1)} fusion(bf16[128,1536]{1,0:T(8,128)(2,1)S(1)} %fusion.60, s32[1024]{0:T(1024)S(1)} %pad_clamp_fusion.1), kind=kCustom, calls=%fused_computation | custom fusion | bytes 3147776 | tf_op jit(solution)/shard_map/jit(_take)/gather | solution.py:170
  132.5 1.6 broadcast_select_fusion
  134.1 39.7 %all_to_all.10 = bf16[4,2,64,1536]{3,2,1,0:T(8,128)(2,1)S(1)} all-to-all(bf16[4,2,64,1536]{3,2,1,0:T(8,128)(2,1)S(1)} %broadcast_select_fusion), channel_id=1, replica_groups=mesh['blk'=8,'exp'=4] {'exp'}, dimensions={0} | all-to-all | bytes 3145728 | tf_op jit(solution)/shard_map/all_to_all | solution.py:173
  173.8 1.1 copy-done.4
  176.0 5.1 %fusion.9 = bf16[4,2,64,1536]{3,2,0,1:T(8,128)(2,1)} fusion(bf16[2,384,1536]{2,1,0:T(8,128)(2,1)S(1)} %copy-done, bf16[2,1536,384]{2,1,0:T(8,128)(2,1)} %param.22, bf16[4,2,64,1536]{3,2,1,0:T(8,128)(2,1)} %copy-done.4, f32[4,2,64,384]{3,2,0,1:T(8,128)S(1)} %fusion.17), kind=kOutput, calls=%fused_computation.18 | convolution fusion | flops 1209925632 | bytes 8650752 | tf_op jit(solution)/shard_map/sjcf,jfd->sjcd/dot_general | solution.py:120
  181.1 2.7 %copy.95 = bf16[4,2,64,1536]{3,2,1,0:T(8,128)(2,1)} copy(bf16[4,2,64,1536]{3,2,0,1:T(8,128)(2,1)} %fusion.9) | data formatting | bytes 3145728 | tf_op jit(solution)/shard_map/convert_element_type | solution.py:122
  183.7 4.3 %all-to-all-start.1 = ((bf16[4,2,64,1536]{3,2,1,0:T(8,128)(2,1)}), bf16[4,2,64,1536]{3,2,1,0:T(8,128)(2,1)}, u32[]{:S(2)}, u32[]{:S(2)}) async-start(bf16[4,2,64,1536]{3,2,1,0:T(8,128)(2,1)} %copy.95), calls=%async_computation.2 | async-start | bytes 3145728 | tf_op jit(solution)/shard_map/all_to_all | solution.py:178
  189.3 35.4 %all-to-all-done.1 = bf16[4,2,64,1536]{3,2,1,0:T(8,128)(2,1)} async-done(((bf16[4,2,64,1536]{3,2,1,0:T(8,128)(2,1)}), bf16[4,2,64,1536]{3,2,1,0:T(8,128)(2,1)}, u32[]{:S(2)}, u32[]{:S(2)}) %all-to-all-start.1) | async-done | bytes 1572896 | tf_op jit(solution)/shard_map/all_to_all | solution.py:178
  224.6 4.5 %gather_fusion.1 = bf16[256,1536]{1,0:T(8,128)(2,1)} fusion(bf16[512,1536]{1,0:T(8,128)(2,1)} %bitcast.47, s32[1024]{0:T(1024)S(1)} %pad_clamp_fusion), kind=kCustom, calls=%fused_computation.1 | custom fusion | bytes 1573888 | tf_op jit(solution)/shard_map/jit(_take)/gather | solution.py:180
  229.1 2.2 gather.15
  231.3 3.9 %multiply_reduce_fusion = bf16[128,1536]{1,0:T(8,128)(2,1)} fusion(bf16[128,2,1536]{2,1,0:T(2,128)(2,1)S(1)} %gather.15, pred[128,2]{1,0:T(8,128)(4,1)S(1)} %copy.91, f32[128,2]{1,0:T(8,128)S(1)} %copy.97), kind=kLoop, calls=%fused_computation.24 | loop fusion | flops 1376256 | bytes 1180928 | tf_op jit(solution)/shard_map/reduce_sum | solution.py:181
  (99 shorter events, 16.2 us)
Async XLA Ops:
  7.2 168.8 %copy-start = (bf16[2,384,1536]{2,1,0:T(8,128)(2,1)S(1)}, bf16[2,384,1536]{2,1,0:T(8,128)(2,1)}, u32[]{:S(2)}) copy-start(bf16[2,384,1536]{2,1,0:T(8,128)(2,1)} %param.23) | copy-start | bytes 7077892
  7.2 44.2 %copy-start.13 = (f32[1536]{0:T(1024)S(1)}, f32[1536]{0:T(1024)}, u32[]{:S(2)}) copy-start(f32[1536]{0:T(1024)} %param.14) | copy-start | bytes 18436
  7.2 44.2 %copy-start.11 = (bf16[1536,128]{1,0:T(8,128)(2,1)S(1)}, bf16[1536,128]{1,0:T(8,128)(2,1)}, u32[]{:S(2)}) copy-start(bf16[1536,128]{1,0:T(8,128)(2,1)} %param.16) | copy-start | bytes 1179652
  7.2 42.2 %all-gather.4.cloned.1.call-start = ((), (), s32[]{:S(2)}) async-start(), calls=%async_computation.3 | async-start | bytes 1966080 | tf_op jit(solution)/shard_map/all_gather | solution.py:142
  7.9 77.4 %all-gather.6.cloned.1.call-start = ((), (), s32[]{:S(2)}) async-start(), calls=%async_computation.5 | async-start | bytes 1179648 | tf_op jit(solution)/shard_map/all_gather | solution.py:57
  49.4 1.9 copy-start.2
  51.4 1.6 copy-start.14
  51.4 1.7 copy-start.12
  52.9 74.3 %reduce-scatter.2.cloned.1.call-start = ((), (), s32[]{:S(2)}) async-start(), calls=%async_computation.4 | async-start | bytes 1966080 | tf_op jit(solution)/shard_map/reduce_scatter | solution.py:156
  53.0 5.5 %copy-start.3 = (bf16[4,128,1536]{2,1,0:T(8,128)(2,1)S(1)}, bf16[4,128,1536]{2,1,0:T(8,128)(2,1)}, u32[]{:S(2)}) copy-start(bf16[4,128,1536]{2,1,0:T(8,128)(2,1)} %all-gather.4.cloned.1.call-done) | copy-start | bytes 4718596
  53.1 5.5 %copy-start.10 = (bf16[1536,384]{1,0:T(8,128)(2,1)S(1)}, bf16[1536,384]{1,0:T(8,128)(2,1)}, u32[]{:S(2)}) copy-start(bf16[1536,384]{1,0:T(8,128)(2,1)} %param.15) | copy-start | bytes 3538948
  55.9 10.0 %collective-permute-start = (bf16[4,128,1,128]{3,1,0,2:T(8,128)(2,1)}, bf16[4,128,1,128]{3,1,0,2:T(8,128)(2,1)S(1)}, u32[]{:S(2)}, u32[]{:S(2)}) collective-permute-start(bf16[4,128,1,128]{3,1,0,2:T(8,128)(2,1)} %bitcast.9), channel_id=1, source_target_pairs={{0,4},{4,8},{8,12},{12,16},{16,20},{20,24},{24,28},{28,0},{1,5},{5... | collective-permute-start | bytes 393224 | tf_op jit(solution)/shard_map/ppermute | solution.py:65
  55.9 10.9 %collective-permute-start.1 = (bf16[4,128,1,128]{3,1,0,2:T(8,128)(2,1)}, bf16[4,128,1,128]{3,1,0,2:T(8,128)(2,1)S(1)}, u32[]{:S(2)}, u32[]{:S(2)}) collective-permute-start(bf16[4,128,1,128]{3,1,0,2:T(8,128)(2,1)} %bitcast.9), channel_id=1, source_target_pairs={{0,28},{4,0},{8,4},{12,8},{16,12},{20,16},{24,20},{28,24},{1,29},{... | collective-permute-start | bytes 393224 | tf_op jit(solution)/shard_map/ppermute | solution.py:68
  63.4 1.0 copy-start.6
  66.0 5.5 %collective-permute-start.2 = (bf16[4,128,1,128]{3,1,0,2:T(8,128)(2,1)S(1)}, bf16[4,128,1,128]{3,1,0,2:T(8,128)(2,1)}, u32[]{:S(2)}, u32[]{:S(2)}) collective-permute-start(bf16[4,128,1,128]{3,1,0,2:T(8,128)(2,1)S(1)} %collective-permute-done), channel_id=1, source_target_pairs={{0,4},{4,8},{8,12},{12,16},{16,20},{20,24},{24,28},{28,0},{1,5},{5... | collective-permute-start | bytes 393224 | tf_op jit(solution)/shard_map/ppermute | solution.py:65
  66.9 6.4 %collective-permute-start.3 = (bf16[4,128,1,128]{3,1,0,2:T(8,128)(2,1)S(1)}, bf16[4,128,1,128]{3,1,0,2:T(8,128)(2,1)}, u32[]{:S(2)}, u32[]{:S(2)}) collective-permute-start(bf16[4,128,1,128]{3,1,0,2:T(8,128)(2,1)S(1)} %collective-permute-done.1), channel_id=1, source_target_pairs={{0,28},{4,0},{8,4},{12,8},{16,12},{20,16},{24,20},{28,24},{1,29},{... | collective-permute-start | bytes 393224 | tf_op jit(solution)/shard_map/ppermute | solution.py:68
  72.5 5.6 %collective-permute-start.4 = (bf16[4,128,1,128]{3,1,0,2:T(8,128)(2,1)}, bf16[4,128,1,128]{3,1,0,2:T(8,128)(2,1)S(1)}, u32[]{:S(2)}, u32[]{:S(2)}) collective-permute-start(bf16[4,128,1,128]{3,1,0,2:T(8,128)(2,1)} %collective-permute-done.2), channel_id=1, source_target_pairs={{0,4},{4,8},{8,12},{12,16},{16,20},{20,24},{24,28},{28,0},{1,5},{5... | collective-permute-start | bytes 393224 | tf_op jit(solution)/shard_map/ppermute | solution.py:65
  74.3 5.9 %collective-permute-start.5 = (bf16[4,128,1,128]{3,1,0,2:T(8,128)(2,1)}, bf16[4,128,1,128]{3,1,0,2:T(8,128)(2,1)S(1)}, u32[]{:S(2)}, u32[]{:S(2)}) collective-permute-start(bf16[4,128,1,128]{3,1,0,2:T(8,128)(2,1)} %collective-permute-done.3), channel_id=1, source_target_pairs={{0,28},{4,0},{8,4},{12,8},{16,12},{20,16},{24,20},{28,24},{1,29},{... | collective-permute-start | bytes 393224 | tf_op jit(solution)/shard_map/ppermute | solution.py:68
  78.2 5.4 %collective-permute-start.6 = (bf16[4,128,1,128]{3,1,0,2:T(8,128)(2,1)S(1)}, bf16[4,128,1,128]{3,1,0,2:T(8,128)(2,1)}, u32[]{:S(2)}, u32[]{:S(2)}) collective-permute-start(bf16[4,128,1,128]{3,1,0,2:T(8,128)(2,1)S(1)} %collective-permute-done.4), channel_id=1, source_target_pairs={{0,4},{4,8},{8,12},{12,16},{16,20},{20,24},{24,28},{28,0},{1,5},{5... | collective-permute-start | bytes 393224 | tf_op jit(solution)/shard_map/ppermute | solution.py:65
  85.4 2.9 %copy-start.7 = (bf16[4,1024,128]{1,2,0:T(8,128)(2,1)S(1)}, bf16[4,1024,128]{1,2,0:T(8,128)(2,1)}, u32[]{:S(2)}) copy-start(bf16[4,1024,128]{1,2,0:T(8,128)(2,1)} %constant_dynamic-update-slice_fusion) | copy-start | bytes 3145732
  88.3 1.5 copy-start.5
  92.0 35.2 %copy-start.1 = (bf16[1,128,1536]{2,1,0:T(8,128)(2,1)S(1)}, bf16[1,128,1536]{2,1,0:T(8,128)(2,1)}, u32[]{:S(2)}) copy-start(bf16[1,128,1536]{2,1,0:T(8,128)(2,1)} %param.13) | copy-start | bytes 1179652
  94.1 34.3 %copy-start.8 = (f32[1536]{0:T(1024)S(1)}, f32[1536]{0:T(1024)}, u32[]{:S(2)}) copy-start(f32[1536]{0:T(1024)} %param.20) | copy-start | bytes 18436
  134.1 40.8 %copy-start.9 = (bf16[2,1536,384]{2,1,0:T(8,128)(2,1)S(1)}, bf16[2,1536,384]{2,1,0:T(8,128)(2,1)}, u32[]{:S(2)}) copy-start(bf16[2,1536,384]{2,1,0:T(8,128)(2,1)} %param.21) | copy-start | bytes 7077892
  173.8 1.1 copy-start.4
  183.7 40.9 %all-to-all-start.1 = ((bf16[4,2,64,1536]{3,2,1,0:T(8,128)(2,1)}), bf16[4,2,64,1536]{3,2,1,0:T(8,128)(2,1)}, u32[]{:S(2)}, u32[]{:S(2)}) async-start(bf16[4,2,64,1536]{3,2,1,0:T(8,128)(2,1)} %copy.95), calls=%async_computation.2 | async-start | bytes 3145728 | tf_op jit(solution)/shard_map/all_to_all | solution.py:178
Sparse Core Ops, SparseCore 0:
  9.6 39.7 all-gather.3
  53.0 24.0 all-gather.5
  92.1 35.0 reduce-scatter.1
